TPU v7x, 32 devices: a whole 2x2x4 slice. The times are simulated.
32 devices in a mesh: tile: 8 (over z, x), lev: 4 (over y, core).
Axes of the slice: x: 2, y: 2, z: 4, core: 2. Of those that a mesh axis runs over, the one named last changes fastest.
Arguments:
- ocean_state: bfloat16 [4, 128, 256, 128], P('lev', 'tile'), may hold values from -6 to 6
- tile_owner: int32 [8, 16], replicated, may hold values from -1 to 63, as said below
- kernel: bfloat16 [7, 7, 128], replicated, may hold values from -0.875 to 0.875
- bias_dw: float32 [128], replicated, may hold values from -3 to 3
- ln_gain: float32 [128], replicated, may hold values from 0.5 to 2
- ln_bias: float32 [128], replicated, may hold values from -3 to 3
- w_in: bfloat16 [128, 512], replicated, may hold values from -0.5 to 0.5
- b_in: float32 [512], replicated, may hold values from -3 to 3
- w_out: bfloat16 [512, 128], replicated, may hold values from -0.25 to 0.25
- b_out: float32 [128], replicated, may hold values from -3 to 3
- layer_scale: float32 [128], replicated, may hold values from 0.3 to 1.5
- w_vert: bfloat16 [5, 128, 128], replicated, may hold values from -0.25 to 0.25
Outputs:
- updated: bfloat16 [64, 4, 256, 128], P('tile', None, 'lev')
Inputs may be any that keep to these rules, and one draw needn't show every extreme that they name: `tile_owner`: every value from 0 to 63 appears exactly once; -1 marks a land tile. Value g names owner g // 8, so every owner receives exactly 8 tiles. No latitude row sends more than 2 tiles to one owner, and in every draw some row sends exactly 2 to some owner.
All inputs are finite; a program needn't handle non-finite values.
Results may differ from a plain program's by a relative error of at most 0.006.
Values may be sent and summed in bfloat16 or wider, within the bound.
A program may use at most 64 MiB of HBM per device.

v0:
```python
import math

import jax
import jax.numpy as jnp
from jax import lax
from jax.sharding import PartitionSpec as P

CAP = 2


def padded_2(cells, sides, width):
    for axis, dim in sides:
        count = lax.axis_size(axis)
        ends = count - 1
        head = lax.slice_in_dim(cells, 0, width, axis=dim)
        tail = lax.slice_in_dim(cells, cells.shape[dim] - width, cells.shape[dim], axis=dim)
        cells = jnp.concatenate(
            [
                lax.ppermute(tail, axis, [(i, (i + 1) % count) for i in range(ends)]),
                cells,
                lax.ppermute(head, axis, [((i + 1) % count, i) for i in range(ends)]),
            ],
            axis=dim,
        )
    return cells


def depthwise(padded, kernel, bias_dw, rows, cols):
    total = jnp.zeros(padded.shape[:-3] + (rows, cols, padded.shape[-1]), jnp.float32) + bias_dw
    for i in range(7):
        for j in range(7):
            total = total + padded[..., i : i + rows, j : j + cols, :].astype(jnp.float32) * kernel[
                i, j
            ].astype(jnp.float32)
    return total.astype(jnp.bfloat16)


def feed_forward(conv_rows, input_rows, ln_gain, ln_bias, w_in, b_in, w_out, b_out, layer_scale):
    values = conv_rows.astype(jnp.float32)
    centre = jnp.mean(values, axis=-1, keepdims=True)
    spread = jnp.mean((values - centre) ** 2, axis=-1, keepdims=True)
    normed = ((values - centre) / jnp.sqrt(spread + 1e-06) * ln_gain + ln_bias).astype(jnp.bfloat16)
    hidden = jax.nn.gelu(
        jnp.dot(normed, w_in, preferred_element_type=jnp.float32) + b_in, approximate=False
    ).astype(jnp.bfloat16)
    branch = jnp.dot(hidden, w_out, preferred_element_type=jnp.float32) + b_out
    return (input_rows.astype(jnp.float32) + layer_scale * branch).astype(jnp.bfloat16)


def pointwise(tile_conv, tile_input, params):
    out_shape = tile_conv.shape
    channels = out_shape[-1]
    conv_rows = tile_conv.reshape(-1, channels)
    input_rows = tile_input.reshape(-1, channels)
    row_count = conv_rows.shape[0]
    block_rows = math.gcd(row_count, 1024)
    block_count = row_count // block_rows

    def apply_block(blocks):
        return feed_forward(blocks[0], blocks[1], *params)

    result = lax.map(
        apply_block,
        (
            conv_rows.reshape(block_count, block_rows, channels),
            input_rows.reshape(block_count, block_rows, channels),
        ),
    )
    return result.reshape(out_shape)


def vertical(block_mid, w_vert):
    level_count = block_mid.shape[-3]
    widths = [(0, 0)] * (block_mid.ndim - 3) + [(2, 2), (0, 0), (0, 0)]
    level_pad = jnp.pad(block_mid, widths)
    channels = block_mid.shape[-1]
    total = block_mid.astype(jnp.float32)
    for k in range(5):
        taken = level_pad[..., k : k + level_count, :, :].reshape(-1, channels)
        total = total + jnp.dot(taken, w_vert[k], preferred_element_type=jnp.float32).reshape(
            block_mid.shape
        )
    return total.astype(jnp.bfloat16)


def to_columns(block_mid, w_vert):
    return vertical(
        lax.all_to_all(block_mid, "lev", split_axis=2, concat_axis=1, tiled=True), w_vert
    )


def body(
    ocean_state,
    tile_owner,
    kernel,
    bias_dw,
    ln_gain,
    ln_bias,
    w_in,
    b_in,
    w_out,
    b_out,
    layer_scale,
    w_vert,
):
    tile_count = lax.axis_size("tile")
    band_index = lax.axis_index("tile")
    local_levels, tile_side, lon_cells, channels = ocean_state.shape
    lon_tiles = tile_owner.shape[1]
    per_owner = tile_owner.shape[0]
    tile_cells = tile_side * tile_side
    params = (ln_gain, ln_bias, w_in, b_in, w_out, b_out, layer_scale)
    dest_all = jnp.where(tile_owner >= 0, tile_owner // per_owner, -1)
    same_dest = (dest_all[:, :, None] == dest_all[:, None, :]) & (tile_owner[:, :, None] >= 0)
    positions = jnp.arange(lon_tiles, dtype=jnp.int32)
    earlier = positions[None, :] < positions[:, None]
    rank_all = jnp.sum((same_dest & earlier[None]).astype(jnp.int32), axis=2)
    my_owner = lax.dynamic_index_in_dim(tile_owner, band_index, 0, keepdims=False)
    my_dest = lax.dynamic_index_in_dim(dest_all, band_index, 0, keepdims=False)
    my_rank = lax.dynamic_index_in_dim(rank_all, band_index, 0, keepdims=False)
    wet_cols = jnp.repeat(my_owner >= 0, tile_side)
    masked = jnp.where(wet_cols[None, None, :, None], ocean_state, jnp.zeros((), ocean_state.dtype))
    padded = padded_2(masked, (("tile", 1),), 3)
    padded = jnp.concatenate([padded[:, :, -3:], padded, padded[:, :, :3]], axis=2)
    conv_out = depthwise(padded, kernel, bias_dw, tile_side, lon_cells)

    def to_tiles(field_in):
        shaped = field_in.reshape(
            local_levels, tile_side, lon_tiles, tile_side, channels
        ).transpose(2, 0, 1, 3, 4)
        return shaped.reshape(lon_tiles, local_levels, tile_cells, channels)

    slot_ids = jnp.arange(tile_count * CAP, dtype=jnp.int32)
    match_table = (my_dest[None, :] == (slot_ids // CAP)[:, None]) & (
        my_rank[None, :] == (slot_ids % CAP)[:, None]
    )
    pick_index = jnp.argmax(match_table.astype(jnp.int32), axis=1)
    present = jnp.any(match_table, axis=1)
    owner_flat = tile_owner.reshape(-1)
    target = band_index * per_owner + jnp.arange(per_owner, dtype=jnp.int32)
    hit_table = (owner_flat[None, :] == target[:, None]).astype(jnp.int32)
    src_flat = jnp.argmax(hit_table, axis=1)
    src_band = src_flat // lon_tiles
    src_rank = rank_all.reshape(-1)[src_flat]
    recv_index = src_band * CAP + src_rank
    band_mid = pointwise(to_tiles(conv_out), to_tiles(masked), params)
    selected = band_mid[pick_index]
    selected = jnp.where(present[:, None, None, None], selected, jnp.zeros((), selected.dtype))
    received = lax.all_to_all(
        selected.reshape(tile_count, CAP, local_levels, tile_cells, channels),
        "tile",
        split_axis=0,
        concat_axis=0,
        tiled=True,
    )
    block_mid = received.reshape(tile_count * CAP, received.shape[2], received.shape[3], channels)[
        recv_index
    ]
    return to_columns(block_mid, w_vert)


def solution(mesh):
    return jax.shard_map(
        body,
        mesh=mesh,
        in_specs=(
            P("lev", "tile", None, None),
            P(),
            P(),
            P(),
            P(),
            P(),
            P(),
            P(),
            P(),
            P(),
            P(),
            P(),
        ),
        out_specs=P("tile", None, "lev", None),
        check_vma=False,
    )
```

profile of v0, /device:TPU:0, one launch (start us, length us, event | category | flops | bytes accessed | tf_op | source)
XLA Modules:
  0.0 116.9 jit_solution(14885101207245512416)
XLA Ops:
  0.0 0.8 compare_bitcast_fusion
  0.8 0.1 broadcast_in_dim.43
  0.9 1.4 %broadcast_select_fusion = bf16[1,16,256,128]{3,2,1,0:T(8,128)(2,1)S(1)} fusion(bf16[1,16,256,128]{3,2,1,0:T(8,128)(2,1)} %param.14, pred[256]{0:T(512)(128)(4,1)S(1)} %broadcast_in_dim.43), kind=kLoop, calls=%fused_computation.134 | loop fusion | flops 524288 | bytes 2097408 | tf_op jit(solution)/shard_map/jit(_where)/select_n | solution.py:122
  2.3 0.8 fusion.124
  3.1 4.8 %collective-permute-start = (bf16[1,3,256,128]{3,2,1,0:T(8,128)(2,1)}, bf16[1,3,256,128]{3,2,1,0:T(8,128)(2,1)S(1)}, u32[]{:S(2)}, u32[]{:S(2)}) collective-permute-start(bf16[1,3,256,128]{3,2,1,0:T(8,128)(2,1)} %get-tuple-element.91), channel_id=1, source_target_pairs={{0,4},{4,8},{8,12},{12,16},{16,20},{20,24},{24,28},{1,5},{5,9},{9,... | collective-permute-start | bytes 589832 | tf_op jit(solution)/shard_map/ppermute | solution.py:19
  8.0 1.3 %collective-permute-start.1 = (bf16[1,3,256,128]{3,2,1,0:T(8,128)(2,1)}, bf16[1,3,256,128]{3,2,1,0:T(8,128)(2,1)S(1)}, u32[]{:S(2)}, u32[]{:S(2)}) collective-permute-start(bf16[1,3,256,128]{3,2,1,0:T(8,128)(2,1)} %get-tuple-element.92), channel_id=1, source_target_pairs={{4,0},{8,4},{12,8},{16,12},{20,16},{24,20},{28,24},{5,1},{9,5},{13... | collective-permute-start | bytes 589832 | tf_op jit(solution)/shard_map/ppermute | solution.py:21
  9.3 0.7 bitcast_convert_fusion.48
  9.9 0.7 bitcast_convert_fusion.47
  10.6 0.3 convert_reduce_fusion.1
  11.0 0.7 iota_reduce_fusion
  11.7 0.8 fusion.118
  12.5 0.3 copy.24
  12.8 0.6 pad_clamp_fusion.2
  13.4 1.3 %broadcast_in_dim.39 = pred[8,2]{1,0:T(8,128)(4,1)} reshape(pred[16]{0:T(512)(128)(4,1)} %fusion.118) | data formatting | bytes 32 | tf_op jit(solution)/shard_map/jit(_where)/broadcast_in_dim | solution.py:148
  15.1 1.3 %collective-permute-done.1 = bf16[1,3,256,128]{3,2,1,0:T(8,128)(2,1)S(1)} collective-permute-done((bf16[1,3,256,128]{3,2,1,0:T(8,128)(2,1)}, bf16[1,3,256,128]{3,2,1,0:T(8,128)(2,1)S(1)}, u32[]{:S(2)}, u32[]{:S(2)}) %collective-permute-start.1) | collective-permute-done | bytes 196640 | tf_op jit(solution)/shard_map/ppermute | solution.py:21
  16.4 5.8 %fusion.100 = (bf16[1,22,259,128]{3,2,1,0:T(8,128)(2,1)S(1)}, bf16[1,22,259,128]{3,2,1,0:T(8,128)(2,1)S(1)}) fusion(bf16[1,3,256,128]{3,2,1,0:T(8,128)(2,1)S(1)} %collective-permute-done.1, bf16[1,16,256,128]{3,2,1,0:T(8,128)(2,1)S(1)} %broadcast_select_fusion, bf16[1,3,256,128]{3,2,1,0:T(8,128)(2,1)S(1)} %collective-permute-done), kind=kLoop, calls=%fused_computation.116 | loop fusion | flops 17504256 | bytes 4359168 | tf_op jit(solution)/shard_map/concatenate | solution.py:124
  22.6 19.8 %add_convert_fusion = bf16[1,16,256,128]{3,2,1,0:T(8,128)(2,1)S(1)} fusion(bf16[1,16,256,128]{3,2,1,0:T(8,128)(2,1)S(1)} %broadcast_select_fusion, bf16[1,3,256,128]{3,2,1,0:T(8,128)(2,1)S(1)} %collective-permute-done.1, bf16[1,3,256,128]{3,2,1,0:T(8,128)(2,1)S(1)} %collective-permute-done, bf16[1,22,259,128]{3,2,1,0:T(8,128)(2,1)S(1)} %get-tuple-element.90, ...), kind=kLoop, calls=%fused_computation.107 | loop fusion | flops 80740352 | bytes 46556160 | tf_op jit(solution)/shard_map/convert_element_type | solution.py:35
  42.5 0.3 copy.25
  42.7 0.5 copy-done.46
  43.4 23.7 %while.10 = (s32[]{:T(128)}, bf16[4,1024,128]{2,1,0:T(8,128)(2,1)S(1)}, bf16[4,1024,128]{2,1,0:T(8,128)(2,1)S(1)}, f32[128]{0:T(128)S(1)}, bf16[4,1024,128]{2,1,...) while((s32[]{:T(128)}, ...), condition=%wide.region_5.6_spmd, body=%wide.region_2.5_spmd.sunk | while | flops 305267712 | bytes 1614973 | solution.py:62
  43.6 0.1 convert_reduce_fusion.3
  43.7 0.4 fusion.140
  44.1 5.3 %fusion.141 = bf16[4,1024,128]{2,1,0:T(8,128)(2,1)S(1)} fusion(bf16[4,1024,128]{2,1,0:T(8,128)(2,1)S(1)} %get-tuple-element.226, s32[]{:T(128)} %get-tuple-element.225, bf16[512,128]{1,0:T(8,128)(2,1)S(1)} %get-tuple-element.246, bf16[128,512]{1,0:T(8,128)(2,1)S(1)} %get-tuple-element.244, f32[512]{0:T(512)S(1)} %get-tuple-element.245, ...), kind=kOutput, calls=%fused_computation.28.clone.1 | convolution fusion | flops 304480256 | bytes 1061888 | tf_op jit(solution)/shard_map/while/body/eval_jaxpr/dot_general | solution.py:46
  49.4 0.2 convert_reduce_fusion.3
  49.6 0.4 fusion.140
  50.0 5.3 %fusion.141 = bf16[4,1024,128]{2,1,0:T(8,128)(2,1)S(1)} fusion(bf16[4,1024,128]{2,1,0:T(8,128)(2,1)S(1)} %get-tuple-element.226, s32[]{:T(128)} %get-tuple-element.225, bf16[512,128]{1,0:T(8,128)(2,1)S(1)} %get-tuple-element.246, bf16[128,512]{1,0:T(8,128)(2,1)S(1)} %get-tuple-element.244, f32[512]{0:T(512)S(1)} %get-tuple-element.245, ...), kind=kOutput, calls=%fused_computation.28.clone.1 | convolution fusion | flops 304480256 | bytes 1061888 | tf_op jit(solution)/shard_map/while/body/eval_jaxpr/dot_general | solution.py:46
  55.3 0.2 convert_reduce_fusion.3
  55.5 0.4 fusion.140
  55.9 5.3 %fusion.141 = bf16[4,1024,128]{2,1,0:T(8,128)(2,1)S(1)} fusion(bf16[4,1024,128]{2,1,0:T(8,128)(2,1)S(1)} %get-tuple-element.226, s32[]{:T(128)} %get-tuple-element.225, bf16[512,128]{1,0:T(8,128)(2,1)S(1)} %get-tuple-element.246, bf16[128,512]{1,0:T(8,128)(2,1)S(1)} %get-tuple-element.244, f32[512]{0:T(512)S(1)} %get-tuple-element.245, ...), kind=kOutput, calls=%fused_computation.28.clone.1 | convolution fusion | flops 304480256 | bytes 1061888 | tf_op jit(solution)/shard_map/while/body/eval_jaxpr/dot_general | solution.py:46
  61.2 0.2 convert_reduce_fusion.3
  61.4 0.4 fusion.140
  61.8 5.3 %fusion.141 = bf16[4,1024,128]{2,1,0:T(8,128)(2,1)S(1)} fusion(bf16[4,1024,128]{2,1,0:T(8,128)(2,1)S(1)} %get-tuple-element.226, s32[]{:T(128)} %get-tuple-element.225, bf16[512,128]{1,0:T(8,128)(2,1)S(1)} %get-tuple-element.246, bf16[128,512]{1,0:T(8,128)(2,1)S(1)} %get-tuple-element.244, f32[512]{0:T(512)S(1)} %get-tuple-element.245, ...), kind=kOutput, calls=%fused_computation.28.clone.1 | convolution fusion | flops 304480256 | bytes 1061888 | tf_op jit(solution)/shard_map/while/body/eval_jaxpr/dot_general | solution.py:46
  67.1 1.0 gather_fusion
  68.1 1.1 broadcast_select_fusion.1
  69.3 7.0 %all-to-all-start = ((bf16[8,2,1,256,128]{4,3,1,2,0:T(8,128)(2,1)}), bf16[8,2,1,256,128]{4,3,1,2,0:T(8,128)(2,1)S(1)}, u32[]{:S(2)}, u32[]{:S(2)}) async-start(bf16[8,2,1,256,128]{4,3,1,2,0:T(8,128)(2,1)} %broadcast_select_fusion.1), calls=%async_computation | async-start | bytes 2097152 | tf_op jit(solution)/shard_map/all_to_all | solution.py:149
  76.3 0.1 eq.75
  76.3 0.1 reshape.573
  76.4 0.7 iota_reduce_fusion.1
  77.1 0.6 gather_fusion.1
  77.8 24.4 %all-to-all-done = bf16[8,2,1,256,128]{4,3,1,2,0:T(8,128)(2,1)S(1)} async-done(((bf16[8,2,1,256,128]{4,3,1,2,0:T(8,128)(2,1)}), bf16[8,2,1,256,128]{4,3,1,2,0:T(8,128)(2,1)S(1)}, u32[]{:S(2)}, u32[]{:S(2)}) %all-to-all-start) | async-done | bytes 1048608 | tf_op jit(solution)/shard_map/all_to_all | solution.py:149
  102.2 0.6 gather_fusion.2
  102.9 0.3 copy.26
  103.2 11.4 %all_to_all.17 = bf16[8,1,256,128]{3,0,1,2:T(8,128)(2,1)S(1)} all-to-all(bf16[8,1,256,128]{3,0,1,2:T(8,128)(2,1)S(1)} %copy.26), channel_id=1, replica_groups=mesh['tile'=8,'lev'=4] {'lev'}, dimensions={2} | all-to-all | bytes 1048576 | tf_op jit(solution)/shard_map/all_to_all | solution.py:88
  114.7 0.3 convolution_add_fusion.3
  115.0 0.3 fusion.109
  115.3 0.3 fusion.101
  115.6 0.3 convolution_add_fusion.1
  115.9 1.1 fusion.102
  (129 shorter events, 0.6 us)
Async XLA Ops:
  0.0 10.6 %copy-start.2 = (s32[8,16]{1,0:T(8,128)S(1)}, s32[8,16]{1,0:T(8,128)}, u32[]{:S(2)}) copy-start(s32[8,16]{1,0:T(8,128)} %param.15) | copy-start | bytes 1540
  0.0 9.3 %copy-start.1 = (bf16[7,7,128]{2,1,0:T(8,128)(2,1)S(1)}, bf16[7,7,128]{2,1,0:T(8,128)(2,1)}, u32[]{:S(2)}) copy-start(bf16[7,7,128]{2,1,0:T(8,128)(2,1)} %param.16) | copy-start | bytes 37636
  3.1 12.0 %collective-permute-start = (bf16[1,3,256,128]{3,2,1,0:T(8,128)(2,1)}, bf16[1,3,256,128]{3,2,1,0:T(8,128)(2,1)S(1)}, u32[]{:S(2)}, u32[]{:S(2)}) collective-permute-start(bf16[1,3,256,128]{3,2,1,0:T(8,128)(2,1)} %get-tuple-element.91), channel_id=1, source_target_pairs={{0,4},{4,8},{8,12},{12,16},{16,20},{20,24},{24,28},{1,5},{5,9},{9,... | collective-permute-start | bytes 589832 | tf_op jit(solution)/shard_map/ppermute | solution.py:19
  8.0 8.5 %collective-permute-start.1 = (bf16[1,3,256,128]{3,2,1,0:T(8,128)(2,1)}, bf16[1,3,256,128]{3,2,1,0:T(8,128)(2,1)S(1)}, u32[]{:S(2)}, u32[]{:S(2)}) collective-permute-start(bf16[1,3,256,128]{3,2,1,0:T(8,128)(2,1)} %get-tuple-element.92), channel_id=1, source_target_pairs={{4,0},{8,4},{12,8},{16,12},{20,16},{24,20},{28,24},{5,1},{9,5},{13... | collective-permute-start | bytes 589832 | tf_op jit(solution)/shard_map/ppermute | solution.py:21
  10.9 1.5 %copy-start.4 = (s32[8,16]{1,0:T(8,128)}, s32[8,16]{1,0:T(8,128)S(1)}, u32[]{:S(2)}) copy-start(s32[8,16]{1,0:T(8,128)S(1)} %convert_reduce_fusion.1) | copy-start | bytes 1540
  14.7 7.5 %copy-start.6 = (f32[128]{0:T(128)S(1)}, f32[128]{0:T(128)}, u32[]{:S(2)}) copy-start(f32[128]{0:T(128)} %get-tuple-element.93) | copy-start | bytes 1540
  14.7 7.5 %copy-start.7 = (f32[128]{0:T(128)S(1)}, f32[128]{0:T(128)}, u32[]{:S(2)}) copy-start(f32[128]{0:T(128)} %get-tuple-element.94) | copy-start | bytes 1540
  14.7 7.5 %copy-start.8 = (f32[128]{0:T(128)S(1)}, f32[128]{0:T(128)}, u32[]{:S(2)}) copy-start(f32[128]{0:T(128)} %get-tuple-element.95) | copy-start | bytes 1540
  14.7 7.5 %copy-start.9 = (f32[128]{0:T(128)S(1)}, f32[128]{0:T(128)}, u32[]{:S(2)}) copy-start(f32[128]{0:T(128)} %get-tuple-element.96) | copy-start | bytes 1540
  14.7 7.5 %copy-start.10 = (f32[128]{0:T(128)S(1)}, f32[128]{0:T(128)}, u32[]{:S(2)}) copy-start(f32[128]{0:T(128)} %get-tuple-element.97) | copy-start | bytes 1540
  14.7 7.5 %copy-start.11 = (f32[128]{0:T(128)S(1)}, f32[128]{0:T(128)}, u32[]{:S(2)}) copy-start(f32[128]{0:T(128)} %get-tuple-element.98) | copy-start | bytes 1540
  14.8 7.5 %copy-start.12 = (f32[128]{0:T(128)S(1)}, f32[128]{0:T(128)}, u32[]{:S(2)}) copy-start(f32[128]{0:T(128)} %get-tuple-element.99) | copy-start | bytes 1540
  14.8 7.5 %copy-start.13 = (f32[128]{0:T(128)S(1)}, f32[128]{0:T(128)}, u32[]{:S(2)}) copy-start(f32[128]{0:T(128)} %get-tuple-element.100) | copy-start | bytes 1540
  14.8 7.5 %copy-start.14 = (f32[128]{0:T(128)S(1)}, f32[128]{0:T(128)}, u32[]{:S(2)}) copy-start(f32[128]{0:T(128)} %get-tuple-element.101) | copy-start | bytes 1540
  14.8 7.5 %copy-start.15 = (f32[128]{0:T(128)S(1)}, f32[128]{0:T(128)}, u32[]{:S(2)}) copy-start(f32[128]{0:T(128)} %get-tuple-element.102) | copy-start | bytes 1540
  14.8 7.5 %copy-start.16 = (f32[128]{0:T(128)S(1)}, f32[128]{0:T(128)}, u32[]{:S(2)}) copy-start(f32[128]{0:T(128)} %get-tuple-element.103) | copy-start | bytes 1540
  14.8 7.5 %copy-start.17 = (f32[128]{0:T(128)S(1)}, f32[128]{0:T(128)}, u32[]{:S(2)}) copy-start(f32[128]{0:T(128)} %get-tuple-element.104) | copy-start | bytes 1540
  14.8 7.5 %copy-start.18 = (f32[128]{0:T(128)S(1)}, f32[128]{0:T(128)}, u32[]{:S(2)}) copy-start(f32[128]{0:T(128)} %get-tuple-element.105) | copy-start | bytes 1540
  14.8 7.5 %copy-start.19 = (f32[128]{0:T(128)S(1)}, f32[128]{0:T(128)}, u32[]{:S(2)}) copy-start(f32[128]{0:T(128)} %get-tuple-element.106) | copy-start | bytes 1540
  14.8 7.5 %copy-start.20 = (f32[128]{0:T(128)S(1)}, f32[128]{0:T(128)}, u32[]{:S(2)}) copy-start(f32[128]{0:T(128)} %get-tuple-element.107) | copy-start | bytes 1540
  14.8 7.5 %copy-start.21 = (f32[128]{0:T(128)S(1)}, f32[128]{0:T(128)}, u32[]{:S(2)}) copy-start(f32[128]{0:T(128)} %get-tuple-element.108) | copy-start | bytes 1540
  14.9 7.5 %copy-start.22 = (f32[128]{0:T(128)S(1)}, f32[128]{0:T(128)}, u32[]{:S(2)}) copy-start(f32[128]{0:T(128)} %get-tuple-element.109) | copy-start | bytes 1540
  14.9 7.5 %copy-start.23 = (f32[128]{0:T(128)S(1)}, f32[128]{0:T(128)}, u32[]{:S(2)}) copy-start(f32[128]{0:T(128)} %get-tuple-element.110) | copy-start | bytes 1540
  14.9 7.5 %copy-start.24 = (f32[128]{0:T(128)S(1)}, f32[128]{0:T(128)}, u32[]{:S(2)}) copy-start(f32[128]{0:T(128)} %get-tuple-element.111) | copy-start | bytes 1540
  14.9 7.5 %copy-start.25 = (f32[128]{0:T(128)S(1)}, f32[128]{0:T(128)}, u32[]{:S(2)}) copy-start(f32[128]{0:T(128)} %get-tuple-element.112) | copy-start | bytes 1540
  14.9 7.5 %copy-start.26 = (f32[128]{0:T(128)S(1)}, f32[128]{0:T(128)}, u32[]{:S(2)}) copy-start(f32[128]{0:T(128)} %get-tuple-element.113) | copy-start | bytes 1540
  14.9 7.5 %copy-start.27 = (f32[128]{0:T(128)S(1)}, f32[128]{0:T(128)}, u32[]{:S(2)}) copy-start(f32[128]{0:T(128)} %get-tuple-element.114) | copy-start | bytes 1540
  14.9 7.5 %copy-start.28 = (f32[128]{0:T(128)S(1)}, f32[128]{0:T(128)}, u32[]{:S(2)}) copy-start(f32[128]{0:T(128)} %get-tuple-element.115) | copy-start | bytes 1540
  14.9 7.5 %copy-start.29 = (f32[128]{0:T(128)S(1)}, f32[128]{0:T(128)}, u32[]{:S(2)}) copy-start(f32[128]{0:T(128)} %get-tuple-element.116) | copy-start | bytes 1540
  14.9 7.5 %copy-start.30 = (f32[128]{0:T(128)S(1)}, f32[128]{0:T(128)}, u32[]{:S(2)}) copy-start(f32[128]{0:T(128)} %get-tuple-element.117) | copy-start | bytes 1540
  14.9 7.5 %copy-start.31 = (f32[128]{0:T(128)S(1)}, f32[128]{0:T(128)}, u32[]{:S(2)}) copy-start(f32[128]{0:T(128)} %get-tuple-element.118) | copy-start | bytes 1540
  15.0 7.5 %copy-start.32 = (f32[128]{0:T(128)S(1)}, f32[128]{0:T(128)}, u32[]{:S(2)}) copy-start(f32[128]{0:T(128)} %get-tuple-element.119) | copy-start | bytes 1540
  15.0 7.5 %copy-start.33 = (f32[128]{0:T(128)S(1)}, f32[128]{0:T(128)}, u32[]{:S(2)}) copy-start(f32[128]{0:T(128)} %get-tuple-element.120) | copy-start | bytes 1540
  15.0 7.5 %copy-start.34 = (f32[128]{0:T(128)S(1)}, f32[128]{0:T(128)}, u32[]{:S(2)}) copy-start(f32[128]{0:T(128)} %get-tuple-element.121) | copy-start | bytes 1540
  15.0 7.5 %copy-start.35 = (f32[128]{0:T(128)S(1)}, f32[128]{0:T(128)}, u32[]{:S(2)}) copy-start(f32[128]{0:T(128)} %get-tuple-element.122) | copy-start | bytes 1540
  15.0 7.5 %copy-start.36 = (f32[128]{0:T(128)S(1)}, f32[128]{0:T(128)}, u32[]{:S(2)}) copy-start(f32[128]{0:T(128)} %get-tuple-element.123) | copy-start | bytes 1540
  15.0 7.5 %copy-start.37 = (f32[128]{0:T(128)S(1)}, f32[128]{0:T(128)}, u32[]{:S(2)}) copy-start(f32[128]{0:T(128)} %get-tuple-element.124) | copy-start | bytes 1540
  15.0 7.5 %copy-start.38 = (f32[128]{0:T(128)S(1)}, f32[128]{0:T(128)}, u32[]{:S(2)}) copy-start(f32[128]{0:T(128)} %get-tuple-element.125) | copy-start | bytes 1540
  15.0 7.5 %copy-start.39 = (f32[128]{0:T(128)S(1)}, f32[128]{0:T(128)}, u32[]{:S(2)}) copy-start(f32[128]{0:T(128)} %get-tuple-element.126) | copy-start | bytes 1540
  15.0 7.5 %copy-start.40 = (f32[128]{0:T(128)S(1)}, f32[128]{0:T(128)}, u32[]{:S(2)}) copy-start(f32[128]{0:T(128)} %get-tuple-element.127) | copy-start | bytes 1540
  15.0 7.5 %copy-start.41 = (f32[128]{0:T(128)S(1)}, f32[128]{0:T(128)}, u32[]{:S(2)}) copy-start(f32[128]{0:T(128)} %get-tuple-element.128) | copy-start | bytes 1540
  15.1 7.5 %copy-start.42 = (f32[128]{0:T(128)S(1)}, f32[128]{0:T(128)}, u32[]{:S(2)}) copy-start(f32[128]{0:T(128)} %get-tuple-element.129) | copy-start | bytes 1540
  15.1 7.5 %copy-start.43 = (f32[128]{0:T(128)S(1)}, f32[128]{0:T(128)}, u32[]{:S(2)}) copy-start(f32[128]{0:T(128)} %get-tuple-element.130) | copy-start | bytes 1540
  15.1 7.5 %copy-start.45 = (f32[128]{0:T(128)S(1)}, f32[128]{0:T(128)}, u32[]{:S(2)}) copy-start(f32[128]{0:T(128)} %param.17) | copy-start | bytes 1540
  69.3 7.0 %copy-start.3 = (s32[8,16]{1,0:T(8,128)S(1)}, s32[8,16]{1,0:T(8,128)}, u32[]{:S(2)}) copy-start(s32[8,16]{1,0:T(8,128)} %param.15) | copy-start | bytes 1540
  69.3 7.1 %copy-start.5 = (s32[8,16]{1,0:T(8,128)S(1)}, s32[8,16]{1,0:T(8,128)}, u32[]{:S(2)}) copy-start(s32[8,16]{1,0:T(8,128)} %copy-done.4) | copy-start | bytes 1540
  69.3 32.9 %all-to-all-start = ((bf16[8,2,1,256,128]{4,3,1,2,0:T(8,128)(2,1)}), bf16[8,2,1,256,128]{4,3,1,2,0:T(8,128)(2,1)S(1)}, u32[]{:S(2)}, u32[]{:S(2)}) async-start(bf16[8,2,1,256,128]{4,3,1,2,0:T(8,128)(2,1)} %broadcast_select_fusion.1), calls=%async_computation | async-start | bytes 2097152 | tf_op jit(solution)/shard_map/all_to_all | solution.py:149
  102.9 11.9 %copy-start = (bf16[5,128,128]{2,1,0:T(8,128)(2,1)S(1)}, bf16[5,128,128]{2,1,0:T(8,128)(2,1)}, u32[]{:S(2)}) copy-start(bf16[5,128,128]{2,1,0:T(8,128)(2,1)} %param.25) | copy-start | bytes 491524
  (8 other events, 7.6 us)
where the time goes:
time: 117 us
  other arithmetic  35.4 us (30%)
  waiting for transfers between devices  25.7 us (22%)
  matrix products  23.5 us (20%)
  starting transfers between devices  13.1 us (11%)
  blocking collectives  11.4 us (10%)
  local copies, waits for them, and re-layouts  6.53 us (6%)
    all_to_all x1, waiting for transfers between devices, body(): lax.all_to_all(selected.reshape(tile_count, CAP, local_levels, tile_cells...  24.4 us
    dot_general x4, matrix products, feed_forward(): branch = jnp.dot(hidden, w_out, preferred_element_type=jnp.float32) + b_out  21.3 us
    convert_element_type x1, other arithmetic, depthwise(): return total.astype(jnp.bfloat16)  19.8 us
    all_to_all x1, blocking collectives, to_columns(): lax.all_to_all(block_mid, 'lev', split_axis=2, concat_axis=1, tiled=True)  11.4 us
    all_to_all x1, starting transfers between devices, body(): lax.all_to_all(selected.reshape(tile_count, CAP, local_levels, tile_cells...  6.98 us
    concatenate x1, other arithmetic, body(): jnp.concatenate([padded[:, :, -3:], padded, padded[:, :, :3]], axis=2)  5.78 us
    ppermute x1, starting transfers between devices, padded_2(): lax.ppermute(tail, axis, [(i, (i + 1) % count) for i in range(ends)])  4.84 us
  transfers between devices with their start and end apart: 3, of which 2 were waited for; matrix products, arithmetic and copies ran while one was open for 6% of the time, Pallas kernels for 0%

commit v1 on v0

v1 whole, which is shorter than its diff:
```python
import jax
import jax.numpy as jnp
from jax import lax
from jax.experimental import pallas as pl
from jax.experimental.pallas import tpu as pltpu
from jax.sharding import PartitionSpec as P

CAP = 2


def block_kernel(
    pick_ref,
    present_ref,
    field_ref,
    taps_ref,
    bias_ref,
    gain_ref,
    shift_ref,
    w_in_ref,
    b_in_ref,
    w_out_ref,
    b_out_ref,
    scale_ref,
    out_ref,
    window,
):
    slot = pl.program_id(0)
    level = pl.program_id(1)
    side = window.shape[0] - 6
    channels = window.shape[2]
    half = side // 2

    @pl.when(present_ref[slot] > 0)
    def _():
        start = pl.multiple_of(pick_ref[slot] * side, side)
        window[...] = field_ref[level, :, pl.ds(start, 2 * side), :].astype(jnp.float32)
        parts = []
        for top in (0, half):
            total = jnp.zeros((half, side, channels), jnp.float32) + bias_ref[...][None]
            for j in range(7):
                column = window[top : top + half + 6, j : j + side, :]
                for i in range(7):
                    tap = taps_ref[i * 7 + j : i * 7 + j + 1, :]
                    total = total + column[i : i + half] * tap[None]
            parts.append(total.reshape(half * side, channels))
        values = jnp.concatenate(parts, axis=0).astype(jnp.bfloat16).astype(jnp.float32)
        centre = jnp.mean(values, axis=-1, keepdims=True)
        offset = values - centre
        spread = jnp.mean(offset * offset, axis=-1, keepdims=True)
        normed = offset * lax.rsqrt(spread + 1e-06) * gain_ref[...] + shift_ref[...]
        wide = (
            jnp.dot(
                normed.astype(jnp.bfloat16), w_in_ref[...], preferred_element_type=jnp.float32
            )
            + b_in_ref[...]
        )
        size = jnp.abs(wide)
        t = 1.0 / (1.0 + 0.231641888 * size)
        poly = t * (
            0.127414796
            + t * (-0.142248368 + t * (0.7107068705 + t * (-0.7265760135 + t * 0.5307027145)))
        )
        tail = poly * jnp.exp(-0.5 * wide * wide)
        hidden = (jnp.maximum(wide, 0.0) - size * tail).astype(jnp.bfloat16)
        branch = (
            jnp.dot(hidden, w_out_ref[...], preferred_element_type=jnp.float32) + b_out_ref[...]
        )
        inner = window[3 : 3 + side, 3 : 3 + side, :].reshape(side * side, channels)
        mid = (inner + scale_ref[...] * branch).astype(jnp.bfloat16)
        out_ref[...] = mid.reshape(out_ref.shape)


def block_slots(padded, pick_index, present, taps, params, tile_count, lev_count):
    levels, rows, width, channels = padded.shape
    side = rows - 6
    share = side * side // lev_count
    slots = pick_index.shape[0]
    bias_dw, ln_gain, ln_bias, w_in, b_in, w_out, b_out, layer_scale = params

    def row(vector):
        return vector.reshape(1, -1)

    operands = (
        padded,
        taps.astype(jnp.float32).reshape(-1, channels),
        row(bias_dw),
        row(ln_gain),
        row(ln_bias),
        w_in,
        row(b_in),
        w_out,
        row(b_out),
        row(layer_scale),
    )

    def whole(operand):
        dims = operand.ndim
        return pl.BlockSpec(operand.shape, lambda s, l, *_: (0,) * dims)

    return pl.pallas_call(
        block_kernel,
        out_shape=jax.ShapeDtypeStruct(
            (tile_count, lev_count, CAP * levels, share, channels), jnp.bfloat16
        ),
        grid_spec=pltpu.PrefetchScalarGridSpec(
            num_scalar_prefetch=2,
            grid=(slots, levels),
            in_specs=[whole(operand) for operand in operands],
            out_specs=pl.BlockSpec(
                (1, lev_count, 1, share, channels),
                lambda s, l, *_: (s // CAP, 0, (s % CAP) * levels + l, 0, 0),
            ),
            scratch_shapes=[pltpu.VMEM((rows, 2 * side, channels), jnp.float32)],
        ),
        compiler_params=pltpu.CompilerParams(vmem_limit_bytes=40 * 1024 * 1024),
    )(pick_index.astype(jnp.int32), present.astype(jnp.int32), *operands)


def padded_rows(cells, axis, width):
    count = lax.axis_size(axis)
    ends = count - 1
    above = lax.ppermute(cells[:, -width:], axis, [(i, i + 1) for i in range(ends)])
    below = lax.ppermute(cells[:, :width], axis, [(i + 1, i) for i in range(ends)])
    return jnp.concatenate([above, cells, below], axis=1)


def vertical(block_mid, w_vert):
    level_count = block_mid.shape[-3]
    widths = [(0, 0)] * (block_mid.ndim - 3) + [(2, 2), (0, 0), (0, 0)]
    level_pad = jnp.pad(block_mid, widths)
    channels = block_mid.shape[-1]
    total = block_mid.astype(jnp.float32)
    for k in range(5):
        taken = level_pad[..., k : k + level_count, :, :].reshape(-1, channels)
        total = total + jnp.dot(taken, w_vert[k], preferred_element_type=jnp.float32).reshape(
            block_mid.shape
        )
    return total.astype(jnp.bfloat16)


def body(
    ocean_state,
    tile_owner,
    kernel,
    bias_dw,
    ln_gain,
    ln_bias,
    w_in,
    b_in,
    w_out,
    b_out,
    layer_scale,
    w_vert,
):
    tile_count = lax.axis_size("tile")
    band_index = lax.axis_index("tile")
    local_levels, tile_side, lon_cells, channels = ocean_state.shape
    lon_tiles = tile_owner.shape[1]
    per_owner = tile_owner.shape[0]
    tile_cells = tile_side * tile_side
    lev_count = lax.axis_size("lev")
    params = (bias_dw, ln_gain, ln_bias, w_in, b_in, w_out, b_out, layer_scale)
    dest_all = jnp.where(tile_owner >= 0, tile_owner // per_owner, -1)
    same_dest = (dest_all[:, :, None] == dest_all[:, None, :]) & (tile_owner[:, :, None] >= 0)
    positions = jnp.arange(lon_tiles, dtype=jnp.int32)
    earlier = positions[None, :] < positions[:, None]
    rank_all = jnp.sum((same_dest & earlier[None]).astype(jnp.int32), axis=2)
    my_owner = lax.dynamic_index_in_dim(tile_owner, band_index, 0, keepdims=False)
    my_dest = lax.dynamic_index_in_dim(dest_all, band_index, 0, keepdims=False)
    my_rank = lax.dynamic_index_in_dim(rank_all, band_index, 0, keepdims=False)
    wet_cols = jnp.repeat(my_owner >= 0, tile_side)
    masked = jnp.where(wet_cols[None, None, :, None], ocean_state, jnp.zeros((), ocean_state.dtype))
    padded = padded_rows(masked, "tile", 3)
    padded = jnp.concatenate(
        [padded[:, :, -3:], padded, padded[:, :, : tile_side - 3]], axis=2
    )

    slot_ids = jnp.arange(tile_count * CAP, dtype=jnp.int32)
    match_table = (my_dest[None, :] == (slot_ids // CAP)[:, None]) & (
        my_rank[None, :] == (slot_ids % CAP)[:, None]
    )
    pick_index = jnp.argmax(match_table.astype(jnp.int32), axis=1)
    present = jnp.any(match_table, axis=1)
    owner_flat = tile_owner.reshape(-1)
    target = band_index * per_owner + jnp.arange(per_owner, dtype=jnp.int32)
    hit_table = (owner_flat[None, :] == target[:, None]).astype(jnp.int32)
    src_flat = jnp.argmax(hit_table, axis=1)
    src_band = src_flat // lon_tiles
    src_rank = rank_all.reshape(-1)[src_flat]
    selected = block_slots(padded, pick_index, present, kernel, params, tile_count, lev_count)
    share = tile_cells // lev_count
    received = lax.all_to_all(
        selected.reshape(tile_count * lev_count, CAP * local_levels, share, channels),
        ("tile", "lev"),
        split_axis=0,
        concat_axis=0,
        tiled=True,
    ).reshape(tile_count, lev_count, CAP, local_levels, share, channels)
    block_mid = received.transpose(0, 2, 1, 3, 4, 5).reshape(
        tile_count * CAP, lev_count * local_levels, share, channels
    )[src_band * CAP + src_rank]
    return vertical(block_mid, w_vert)


def solution(mesh):
    return jax.shard_map(
        body,
        mesh=mesh,
        in_specs=(
            P("lev", "tile", None, None),
            P(),
            P(),
            P(),
            P(),
            P(),
            P(),
            P(),
            P(),
            P(),
            P(),
            P(),
        ),
        out_specs=P("tile", None, "lev", None),
        check_vma=False,
    )
```

time: 117 us -> 72.7 us (0.62)
  other arithmetic: 35.4 us -> 7.96 us
  matrix products: 23.5 us -> 2.19 us
  Pallas kernels: 0 us -> 15.1 us
  blocking collectives: 11.4 us -> 0 us
  local copies, waits for them, and re-layouts: 6.53 us -> 1.98 us
  waiting for transfers between devices: 25.7 us -> 30.2 us
  starting transfers between devices: 13.1 us -> 14.4 us
    dot_general x4 -> x0, matrix products: 21.3 us -> none  [feed_forward(): branch = jnp.dot(hidden, w_out, preferred_element_type=jnp.float32) + b_out]
    convert_element_type x4 -> x1, other arithmetic: 21.1 us -> 0.01 us  [block_slots(): present.astype(jnp.int32)]
    pallas_call x0 -> x1, Pallas kernels: none -> 15.1 us  [block_slots(): pl.pallas_call(block_kernel, out_shape=jax.ShapeDtypeStruct((tile_count,...]
    all_to_all x1 -> x0, blocking collectives: 11.4 us -> none  [to_columns(): lax.all_to_all(block_mid, 'lev', split_axis=2, concat_axis=1, tiled=True)]
    ppermute x2, waiting for transfers between devices: 1.32 us -> 5.55 us  [the longest x1 4.04 us: padded_rows(): lax.ppermute(cells[:, :width], axis, [(i + 1, i) for i in range(ends)])]
    reduce_sum x8 -> x0, other arithmetic: 2.07 us -> none  [the longest x4 1.45 us: feed_forward(): spread = jnp.mean((values - centre) ** 2, axis=-1, keepdims=True)]
    concatenate x1, other arithmetic: 5.78 us -> 3.83 us  [body(): jnp.concatenate([padded[:, :, -3:], padded, padded[:, :, :tile_side - 3]]...]
    gather x3 -> x1, local copies, waits for them, and re-layouts: 2 us -> 0.65 us  [body(): received.transpose(0, 2, 1, 3, 4, 5)]
  transfers between devices with their start and end apart: 3 -> 3, of which waited for: 2 -> 3; matrix products, arithmetic and copies ran while one was open for 6% -> 4% of each run, Pallas kernels for 0% -> 0%
where the time goes in v1:
time: 72.7 us; the launch traced here: 72.2 us
  waiting for transfers between devices  30.2 us (42%)
  Pallas kernels  15.1 us (21%)
  starting transfers between devices  14.4 us (20%)
  other arithmetic  7.96 us (11%)
  matrix products  2.19 us (3%)
  local copies, waits for them, and re-layouts  1.98 us (3%)
    all_to_all x1, waiting for transfers between devices, body(): lax.all_to_all(selected.reshape(tile_count * lev_count, CAP * local_level...  24.7 us
    pallas_call x1, Pallas kernels, block_slots(): pl.pallas_call(block_kernel, out_shape=jax.ShapeDtypeStruct((tile_count,...  15.1 us
    all_to_all x1, starting transfers between devices, body(): lax.all_to_all(selected.reshape(tile_count * lev_count, CAP * local_level...  8.26 us
    ppermute x1, starting transfers between devices, padded_rows(): lax.ppermute(cells[:, -width:], axis, [(i, i + 1) for i in range(ends)])  4.85 us
    ppermute x1, waiting for transfers between devices, padded_rows(): lax.ppermute(cells[:, :width], axis, [(i + 1, i) for i in range(ends)])  4.04 us
    concatenate x1, other arithmetic, body(): jnp.concatenate([padded[:, :, -3:], padded, padded[:, :, :tile_side - 3]]...  3.83 us
    dot_general x5, matrix products, vertical(): jnp.dot(taken, w_vert[k], preferred_element_type=jnp.float32)  2.19 us
    ppermute x1, waiting for transfers between devices, padded_rows(): lax.ppermute(cells[:, -width:], axis, [(i, i + 1) for i in range(ends)])  1.51 us
  transfers between devices with their start and end apart: 3, of which 3 were waited for; matrix products, arithmetic and copies ran while one was open for 4% of the time, Pallas kernels for 0%

profile of v1, /device:TPU:0, one launch (start us, length us, event | category | flops | bytes accessed | tf_op | source)
XLA Modules:
  0.0 72.2 jit_solution(13176667707643771000)
XLA Ops:
  0.0 0.0 copy-start.9
  0.0 0.0 copy-start.10
  0.0 0.8 %compare_bitcast_fusion = pred[16]{0:T(512)(128)(4,1)S(1)} fusion(s32[8,16]{1,0:T(8,128)} %param.13, s32[]{:T(128)S(6)} %select_n.60), kind=kLoop, calls=%fused_computation.45 | loop fusion | flops 16 | bytes 84 | tf_op jit(solution)/shard_map/ge | solution.py:171
  0.8 0.1 broadcast_in_dim.22
  0.8 0.1 broadcast_in_dim.23
  0.9 1.4 %broadcast_select_fusion = bf16[1,16,256,128]{3,2,1,0:T(8,128)(2,1)S(1)} fusion(bf16[1,16,256,128]{3,2,1,0:T(8,128)(2,1)} %param.12, pred[256]{0:T(512)(128)(4,1)S(1)} %broadcast_in_dim.23), kind=kLoop, calls=%fused_computation.14 | loop fusion | flops 524288 | bytes 2097408 | tf_op jit(solution)/shard_map/jit(_where)/select_n | solution.py:172
  2.4 4.9 %collective-permute-start = (bf16[1,3,256,128]{3,2,1,0:T(8,128)(2,1)S(1)}, bf16[1,3,256,128]{3,2,1,0:T(8,128)(2,1)S(1)}, u32[]{:S(2)}, u32[]{:S(2)}) collective-permute-start(bf16[1,3,256,128]{3,2,1,0:T(8,128)(2,1)S(1)} %get-tuple-element.9), channel_id=1, source_target_pairs={{0,4},{4,8},{8,12},{12,16},{16,20},{20,24},{24,28},{1,5},{5,9},{9,... | collective-permute-start | bytes 589832 | tf_op jit(solution)/shard_map/ppermute | solution.py:122
  7.3 1.3 %collective-permute-start.1 = (bf16[1,3,256,128]{3,2,1,0:T(8,128)(2,1)S(1)}, bf16[1,3,256,128]{3,2,1,0:T(8,128)(2,1)S(1)}, u32[]{:S(2)}, u32[]{:S(2)}) collective-permute-start(bf16[1,3,256,128]{3,2,1,0:T(8,128)(2,1)S(1)} %get-tuple-element.10), channel_id=1, source_target_pairs={{4,0},{8,4},{12,8},{16,12},{20,16},{24,20},{28,24},{5,1},{9,5},{13... | collective-permute-start | bytes 589832 | tf_op jit(solution)/shard_map/ppermute | solution.py:123
  8.6 0.0 copy-done.9
  8.6 0.0 copy-start
  8.6 0.0 copy-start.1
  8.7 0.0 copy-start.2
  8.7 0.0 copy-start.3
  8.7 0.0 copy-start.4
  8.7 0.0 copy-start.5
  8.7 0.0 copy-start.6
  8.7 0.0 copy-start.7
  8.7 0.3 convert_reduce_fusion
  9.0 0.2 fusion.15
  9.2 0.0 copy-done.10
  9.3 0.7 iota_reduce_fusion
  10.0 1.5 %collective-permute-done = bf16[1,3,256,128]{3,2,1,0:T(8,128)(2,1)S(1)} collective-permute-done((bf16[1,3,256,128]{3,2,1,0:T(8,128)(2,1)S(1)}, bf16[1,3,256,128]{3,2,1,0:T(8,128)(2,1)S(1)}, u32[]{:S(2)}, u32[]{:S(2)}) %collective-permute-start) | collective-permute-done | bytes 196640 | tf_op jit(solution)/shard_map/ppermute | solution.py:122
  11.5 4.0 %collective-permute-done.1 = bf16[1,3,256,128]{3,2,1,0:T(8,128)(2,1)S(1)} collective-permute-done((bf16[1,3,256,128]{3,2,1,0:T(8,128)(2,1)S(1)}, bf16[1,3,256,128]{3,2,1,0:T(8,128)(2,1)S(1)}, u32[]{:S(2)}, u32[]{:S(2)}) %collective-permute-start.1) | collective-permute-done | bytes 196640 | tf_op jit(solution)/shard_map/ppermute | solution.py:123
  15.5 3.8 %fusion.field_ref = bf16[1,22,272,128]{3,2,1,0:T(8,128)(2,1)S(1)} fusion(bf16[1,3,256,128]{3,2,1,0:T(8,128)(2,1)S(1)} %collective-permute-done.1, bf16[1,16,256,128]{3,2,1,0:T(8,128)(2,1)S(1)} %broadcast_select_fusion, bf16[1,3,256,128]{3,2,1,0:T(8,128)(2,1)S(1)} %collective-permute-done), kind=kLoop, calls=%fused_computation.3 | loop fusion | flops 13787136 | bytes 2973696 | tf_op jit(solution)/shard_map/concatenate | solution.py:174
  19.4 0.0 copy-done
  19.4 0.0 copy-done.1
  19.4 0.0 copy-done.2
  19.4 0.0 copy-done.3
  19.4 0.0 copy-done.4
  19.4 0.0 copy-done.5
  19.4 0.0 copy-done.6
  19.4 0.0 copy-done.7
  19.4 15.1 %shard_map.118 = bf16[8,4,2,64,128]{4,3,2,1,0:T(8,128)(2,1)} custom-call(s32[16]{0:T(128)S(1)} %get-tuple-element.7.pick_ref, s32[16]{0:T(128)S(1)} %convert_element_type.23.present_ref, bf16[1,22,272,128]{3,2,1,0:T(8,128)(2,1)S(1)} %fusion.field_ref, f32[49,128]{1,0:T(8,128)S(1)} %reshape.116.taps_ref, f32[1,128]{1,0:T(1,128)S(1)} %bitcast.58, ...), custom_call_target="tpu_custom_call" | custom-call | tf_op jit(solution)/shard_map/pallas_call | solution.py:100
  34.5 8.3 %all-to-all-start = ((bf16[32,2,64,128]{3,2,1,0:T(8,128)(2,1)}), bf16[32,2,64,128]{3,2,1,0:T(8,128)(2,1)S(1)}, u32[]{:S(2)}, u32[]{:S(2)}) async-start(bf16[32,2,64,128]{3,2,1,0:T(8,128)(2,1)} %bitcast.9), calls=%async_computation | async-start | bytes 2097152 | tf_op jit(solution)/shard_map/all_to_all | solution.py:192
  42.8 0.1 eq.75
  42.9 0.1 reshape.114
  43.0 0.7 iota_reduce_fusion.1
  43.7 0.6 gather_fusion
  44.3 24.7 %all-to-all-done = bf16[32,2,64,128]{3,2,1,0:T(8,128)(2,1)S(1)} async-done(((bf16[32,2,64,128]{3,2,1,0:T(8,128)(2,1)}), bf16[32,2,64,128]{3,2,1,0:T(8,128)(2,1)S(1)}, u32[]{:S(2)}, u32[]{:S(2)}) %all-to-all-start) | async-done | bytes 1048608 | tf_op jit(solution)/shard_map/all_to_all | solution.py:192
  69.0 0.0 copy-start.8
  69.0 0.1 copy.14
  69.1 0.7 gather_fusion.1
  69.8 0.2 copy-done.8
  69.9 0.3 convolution_add_fusion.3
  70.2 0.3 fusion.6
  70.5 0.3 fusion.2
  70.8 0.3 convolution_add_fusion.1
  71.1 1.1 %fusion.3 = bf16[8,4,64,128]{3,2,1,0:T(8,128)(2,1)} fusion(f32[8,4,64,128]{3,2,1,0:T(8,128)S(1)} %convolution_add_fusion.1, bf16[8,4,64,128]{3,2,1,0:T(8,128)(2,1)S(1)} %gather_fusion.1, bf16[5,128,128]{2,1,0:T(8,128)(2,1)S(1)} %copy-done.8), kind=kOutput, calls=%fused_computation.13 | convolution fusion | flops 34078720 | bytes 2129920 | tf_op jit(solution)/shard_map/dot_general | solution.py:135
  (13 shorter events, 0.1 us)
Async XLA Ops:
  0.0 8.6 %copy-start.9 = (s32[8,16]{1,0:T(8,128)S(1)}, s32[8,16]{1,0:T(8,128)}, u32[]{:S(2)}) copy-start(s32[8,16]{1,0:T(8,128)} %param.13) | copy-start | bytes 1540
  0.0 9.2 %copy-start.10 = (bf16[7,7,128]{2,1,0:T(8,128)(2,1)S(1)}, bf16[7,7,128]{2,1,0:T(8,128)(2,1)}, u32[]{:S(2)}) copy-start(bf16[7,7,128]{2,1,0:T(8,128)(2,1)} %param.14) | copy-start | bytes 37636
  2.4 9.1 %collective-permute-start = (bf16[1,3,256,128]{3,2,1,0:T(8,128)(2,1)S(1)}, bf16[1,3,256,128]{3,2,1,0:T(8,128)(2,1)S(1)}, u32[]{:S(2)}, u32[]{:S(2)}) collective-permute-start(bf16[1,3,256,128]{3,2,1,0:T(8,128)(2,1)S(1)} %get-tuple-element.9), channel_id=1, source_target_pairs={{0,4},{4,8},{8,12},{12,16},{16,20},{20,24},{24,28},{1,5},{5,9},{9,... | collective-permute-start | bytes 589832 | tf_op jit(solution)/shard_map/ppermute | solution.py:122
  7.3 8.3 %collective-permute-start.1 = (bf16[1,3,256,128]{3,2,1,0:T(8,128)(2,1)S(1)}, bf16[1,3,256,128]{3,2,1,0:T(8,128)(2,1)S(1)}, u32[]{:S(2)}, u32[]{:S(2)}) collective-permute-start(bf16[1,3,256,128]{3,2,1,0:T(8,128)(2,1)S(1)} %get-tuple-element.10), channel_id=1, source_target_pairs={{4,0},{8,4},{12,8},{16,12},{20,16},{24,20},{28,24},{5,1},{9,5},{13... | collective-permute-start | bytes 589832 | tf_op jit(solution)/shard_map/ppermute | solution.py:123
  8.6 10.7 %copy-start = (bf16[128,512]{1,0:T(8,128)(2,1)S(1)}, bf16[128,512]{1,0:T(8,128)(2,1)}, u32[]{:S(2)}) copy-start(bf16[128,512]{1,0:T(8,128)(2,1)} %w_in_ref.1) | copy-start | bytes 393220
  8.6 10.7 %copy-start.1 = (bf16[512,128]{1,0:T(8,128)(2,1)S(1)}, bf16[512,128]{1,0:T(8,128)(2,1)}, u32[]{:S(2)}) copy-start(bf16[512,128]{1,0:T(8,128)(2,1)} %w_out_ref.1) | copy-start | bytes 393220
  8.7 10.7 %copy-start.2 = (f32[512]{0:T(512)S(1)}, f32[512]{0:T(512)}, u32[]{:S(2)}) copy-start(f32[512]{0:T(512)} %param.19) | copy-start | bytes 6148
  8.7 10.7 %copy-start.3 = (f32[128]{0:T(128)S(1)}, f32[128]{0:T(128)}, u32[]{:S(2)}) copy-start(f32[128]{0:T(128)} %param.15) | copy-start | bytes 1540
  8.7 10.7 %copy-start.4 = (f32[128]{0:T(128)S(1)}, f32[128]{0:T(128)}, u32[]{:S(2)}) copy-start(f32[128]{0:T(128)} %param.16) | copy-start | bytes 1540
  8.7 10.7 %copy-start.5 = (f32[128]{0:T(128)S(1)}, f32[128]{0:T(128)}, u32[]{:S(2)}) copy-start(f32[128]{0:T(128)} %param.17) | copy-start | bytes 1540
  8.7 10.7 %copy-start.6 = (f32[128]{0:T(128)S(1)}, f32[128]{0:T(128)}, u32[]{:S(2)}) copy-start(f32[128]{0:T(128)} %param.21) | copy-start | bytes 1540
  8.7 10.7 %copy-start.7 = (f32[128]{0:T(128)S(1)}, f32[128]{0:T(128)}, u32[]{:S(2)}) copy-start(f32[128]{0:T(128)} %param.22) | copy-start | bytes 1540
  34.5 34.5 %all-to-all-start = ((bf16[32,2,64,128]{3,2,1,0:T(8,128)(2,1)}), bf16[32,2,64,128]{3,2,1,0:T(8,128)(2,1)S(1)}, u32[]{:S(2)}, u32[]{:S(2)}) async-start(bf16[32,2,64,128]{3,2,1,0:T(8,128)(2,1)} %bitcast.9), calls=%async_computation | async-start | bytes 2097152 | tf_op jit(solution)/shard_map/all_to_all | solution.py:192
  69.0 0.9 %copy-start.8 = (bf16[5,128,128]{2,1,0:T(8,128)(2,1)S(1)}, bf16[5,128,128]{2,1,0:T(8,128)(2,1)}, u32[]{:S(2)}) copy-start(bf16[5,128,128]{2,1,0:T(8,128)(2,1)} %param.23) | copy-start | bytes 491524
